TPU v7x, 128 devices: a whole 4x4x4 slice. The times are simulated.
128 devices in a mesh: hi: 8 (over x_hi, z), lo: 16 (over y, x_lo, core).
Axes of the slice: x: 4 (x_hi: 2, x_lo: 2; x = x_hi * 2 + x_lo), y: 4, z: 4, core: 2. Of those that a mesh axis runs over, the one named last changes fastest.
Arguments:
- amplitudes: float32 [2, 128, 262144], P(None, ('hi', 'lo')), may hold values from -20 to 20
- gate_picks: int32 [2, 25], replicated, may hold values from 0 to 2
- pair_qubits: int32 [2, 10, 2], replicated, may hold values from 0 to 24, as said below
- angles: float32 [2, 10], replicated, may hold values from -3.140625 to 3.140625
Outputs:
- final_state: float32 [2, 128, 262144], P(None, ('hi', 'lo'))
- marginal: float32 [128], replicated
Inputs may be any that keep to these rules, and one draw needn't show every extreme that they name: `pair_qubits`: in each layer the 20 qubits named are all different; qubit 0 and qubit 25 - 1 are named in every layer.
All inputs are finite; a program needn't handle non-finite values.
Results may differ from a plain program's by a relative error of at most 0.0001.
Values sent between devices are 32-bit elements; how exact they have to be, the bound alone decides.
A program may use at most 128 MiB of HBM per device.

v0:
```python
import functools
import math

import jax
import jax.numpy as jnp
from jax import lax
from jax.experimental import pallas as pl
from jax.experimental.pallas import tpu as pltpu
from jax.sharding import PartitionSpec as P

MESH = pl.DeviceIdType.MESH

PHASE_IN = (-2, 4, 5)
PHASE_OUT = (-2, 0, -1)
PHASE_ALL = (1, 1, 0)

ROW_BITS = (0, 4, 5, 2, 3, 1, 6)
CHUNK_QUBITS = (9, 10)
CHUNKS = 4
SIZE = {"x": 4, "y": 4, "z": 4, "c": 2}
DIM = {"x": 0, "y": 1, "z": 2, "c": 3}

ORDER = ("xczy", "yxcz", "zyxc", "czyx")


def coordinates():
    hi, lo = lax.axis_index("hi"), lax.axis_index("lo")
    return {
        "x": (hi // 4) * 2 + (lo // 2) % 2,
        "y": lo // 4,
        "z": hi % 4,
        "c": lo % 2,
    }


def device_at(pos):
    return ((pos["x"] // 2) * 4 + pos["z"], pos["y"] * 4 + (pos["x"] % 2) * 2 + pos["c"])


def moved(pos, **flips):
    return device_at({a: jnp.bitwise_xor(pos[a], flips[a]) if flips.get(a, 0) else pos[a] for a in pos})


def hadamard(tiles):
    tiles = list(tiles)
    step = 1
    while step < len(tiles):
        for i in range(len(tiles)):
            if not i & step:
                a, b = tiles[i], tiles[i + step]
                tiles[i], tiles[i + step] = a + b, a - b
        step *= 2
    return tiles


def choose(table, pick):
    return jnp.where(pick == 0, table[0], jnp.where(pick == 1, table[1], table[2]))


def parity_sign(value):
    value = value ^ (value >> 4)
    value = value ^ (value >> 2)
    value = value ^ (value >> 1)
    return 1.0 - 2.0 * (value & 1).astype(jnp.float32)


def split(value):
    high = value.astype(jnp.bfloat16)
    low = (value - high.astype(jnp.float32)).astype(jnp.bfloat16)
    return jnp.concatenate([high, low], axis=1)


def part(ref, slot, at):
    index = [slot] + [at.get(a, slice(None)) for a in "xyzc"]
    return ref.at[tuple(index)]


def kernel(
    x_hbm,
    picks,
    pairs,
    angles,
    out_hbm,
    marginal_ref,
    st,
    vin,
    vout,
    tab_c,
    tab_s,
    in_c,
    in_s,
    fac_c,
    fac_s,
    work,
    acc,
    lanes_mat,
    rows_mat,
    mass_a,
    mass_b,
    in_sem,
    out_sem,
    send_sem,
    recv_sem,
    last_sem,
    mass_send,
    mass_recv,
):
    pos = coordinates()
    me = lax.axis_index("hi") * 16 + lax.axis_index("lo")

    def load(b):
        rows = pl.ds(b * 16, 16)
        return pltpu.make_async_copy(x_hbm.at[:, rows], vin.at[:, rows], in_sem.at[b])

    for b in range(8):
        load(b).start()

    barrier = pltpu.get_barrier_semaphore()
    flips = [{"z": z, "c": c} for z in range(4) for c in range(2) if z or c]
    flips += [{"x": x, "y": y} for x in range(4) for y in range(4) if x or y]
    for flip in flips:
        pl.semaphore_signal(barrier, inc=1, device_id=moved(pos, **flip), device_id_type=MESH)

    lane = lax.broadcasted_iota(jnp.int32, (8, 128), 1)
    sub = lax.broadcasted_iota(jnp.int32, (8, 128), 0)
    top = sub < 4
    side = jnp.where(top, -1.0, 1.0)
    local_n = lane | ((sub & 3) << 7)
    eighth = math.pi / 4

    lin_in = [choose(PHASE_IN, picks[0, q]) for q in range(25)]
    n_first = local_n | (me << 18)
    turn = jnp.zeros((8, 128), jnp.int32)
    for q in list(range(9)) + list(range(18, 25)):
        turn = turn + ((n_first >> q) & 1) * lin_in[q]
    for k in range(8):
        angle = ((turn + k) & 7).astype(jnp.float32) * eighth
        in_c[k] = jnp.cos(angle)
        in_s[k] = jnp.sin(angle) * side

    def swap(value):
        return pltpu.roll(value, 4, 0)

    def first_rows(i, _):
        xh, z, y = i // 16, (i // 4) % 4, i % 4
        k0 = xh * lin_in[17] + (z // 2) * lin_in[16] + (z % 2) * lin_in[15] + (y // 2) * lin_in[14] + (y % 2) * lin_in[13]
        for xl in range(2):
            for c in range(2):
                m = i * 4 + xl * 2 + c
                k1 = k0 + xl * lin_in[12] + c * lin_in[11]
                tiles = []
                for t in range(2):
                    re = vin[0, m, pl.ds(8 * t, 8)]
                    im = vin[1, m, pl.ds(8 * t, 8)]
                    rre, rim = swap(re), swap(im)
                    for e in range(2):
                        k = (k1 + t * lin_in[10] + e * lin_in[9]) & 7
                        if e == 0:
                            p, pr = jnp.where(top, re, rim), jnp.where(top, im, rre)
                        else:
                            p, pr = jnp.where(top, rre, im), jnp.where(top, rim, re)
                        tiles.append(p * in_c[k] + pr * in_s[k])
                tiles = hadamard(tiles)
                for j in range(CHUNKS):
                    st[j, 2 * xh + xl, y, z, c] = tiles[j]
        return 0

    for b in range(8):
        load(b).wait()
        lax.fori_loop(b * 4, b * 4 + 4, first_rows, 0)

    def walsh_rows(slot, mass=None):
        def pass_xy(i, _):
            z, c = i // 2, i % 2
            tiles = hadamard([st[slot, x, y, z, c] for x in range(4) for y in range(4)])
            for x in range(4):
                for y in range(4):
                    st[slot, x, y, z, c] = tiles[x * 4 + y]
            return 0

        def pass_zc(i, _):
            x, y = i // 4, i % 4
            tiles = hadamard([st[slot, x, y, z, c] for z in range(4) for c in range(2)])
            for z in range(4):
                for c in range(2):
                    tile = tiles[z * 2 + c]
                    st[slot, x, y, z, c] = tile
                    if mass == 0:
                        acc[x, y, z, c] = tile * tile
                    elif mass is not None:
                        acc[x, y, z, c] = acc[x, y, z, c] + tile * tile
            return 0

        lax.fori_loop(0, 8, pass_xy, 0)
        lax.fori_loop(0, 16, pass_zc, 0)

    def slot_of(e, i, j):
        return e * 20 + i * 4 + j

    def half(j, h):
        d = ORDER[j][3]
        width = SIZE[d] // 2
        return d, pl.ds(jnp.bitwise_xor(pos[d] // width, h) * width, width)

    def send_step(e, j, i, h):
        a = ORDER[j][i]
        if i < 3:
            d, piece = half(j, h)
            for flip in range(SIZE[a]):
                target = jnp.bitwise_xor(pos[a], flip) if flip else pos[a]
                src = part(st, slot_of(e, i, j), {a: target, d: piece})
                dst = part(st, slot_of(e, i + 1, j), {a: pos[a], d: piece})
                if flip:
                    pltpu.make_async_remote_copy(
                        src,
                        dst,
                        send_sem.at[e, j, i],
                        recv_sem.at[e, j, i, h],
                        device_id=moved(pos, **{a: flip}),
                        device_id_type=MESH,
                    ).start()
                else:
                    pltpu.make_async_copy(src, dst, recv_sem.at[e, j, i, h]).start()
        else:
            width = SIZE[a] // 2
            for flip in range(h * width, h * width + width):
                target = jnp.bitwise_xor(pos[a], flip) if flip else pos[a]
                src = part(st, slot_of(e, i, j), {a: target})
                dst = part(st, slot_of(e, i + 1, j), {a: pos[a]})
                if flip:
                    pltpu.make_async_remote_copy(
                        src,
                        dst,
                        send_sem.at[e, j, i],
                        last_sem.at[e, j],
                        device_id=moved(pos, **{a: flip}),
                        device_id_type=MESH,
                    ).start()
                else:
                    pltpu.make_async_copy(src, dst, last_sem.at[e, j]).start()

    def arrived_step(e, j, i, h):
        if i < 3:
            d, piece = half(j, h)
            ref = part(st, slot_of(e, i + 1, j), {d: piece})
            pltpu.make_async_copy(ref, ref, recv_sem.at[e, j, i, h]).wait()
        else:
            ref = st.at[slot_of(e, 4, j)]
            pltpu.make_async_copy(ref, ref, last_sem.at[e, j]).wait()

    def sent(e, steps):
        for j in range(CHUNKS):
            for i in steps:
                a = ORDER[j][i]
                ref = part(st, slot_of(e, i, j), {a: pl.ds(0, SIZE[a] * 3 // 4 if SIZE[a] == 4 else 1)})
                pltpu.make_async_copy(ref, ref, send_sem.at[e, j, i]).wait()

    def travel(e):
        for i in range(1, 4):
            for h in (1, 0):
                for j in range(CHUNKS):
                    arrived_step(e, j, i - 1, h)
                    send_step(e, j, i, h)

    pl.semaphore_wait(barrier, len(flips))
    for j in range(CHUNKS):
        walsh_rows(j)
        for h in (1, 0):
            send_step(0, j, 0, h)

    def phase_table(layer, n_base, row_base, linear, constant, scale):
        tile_qubits = [row_base + b for b in ROW_BITS] + list(CHUNK_QUBITS)
        other = [q for q in range(25) if q not in tile_qubits]
        first = [pairs[layer, k, 0] for k in range(10)]
        second = [pairs[layer, k, 1] for k in range(10)]
        theta = [angles[layer, k] for k in range(10)]
        n0 = local_n | n_base
        turns = jnp.full((8, 128), 0, jnp.int32) + constant
        for q in other:
            turns = turns + ((n0 >> q) & 1) * linear[q]
        phase = jnp.zeros((8, 128), jnp.float32)
        for k in range(10):
            both = (n0 >> first[k]) & (n0 >> second[k]) & 1
            phase = phase + theta[k] * both.astype(jnp.float32)
        phase = phase + (turns & 7).astype(jnp.float32) * eighth
        tab_c[0] = jnp.cos(phase) * scale
        tab_s[0] = jnp.sin(phase) * side * scale
        partners = []
        for b, q in enumerate(tile_qubits):
            partner, angle = jnp.int32(31), jnp.float32(0.0)
            for k in range(10):
                is_first, is_second = first[k] == q, second[k] == q
                partner = jnp.where(is_first, second[k], jnp.where(is_second, first[k], partner))
                angle = jnp.where(is_first | is_second, theta[k], angle)
            partners.append(partner)
            own = (linear[q] & 7).astype(jnp.float32) * eighth
            bit = ((n0 >> partner) & 1).astype(jnp.float32)
            zero = own + angle * bit
            fac_c[2 * b] = jnp.cos(zero)
            fac_s[2 * b] = jnp.sin(zero) * side
            one = zero * 0.0 + (own + angle)
            fac_c[2 * b + 1] = jnp.cos(one)
            fac_s[2 * b + 1] = jnp.sin(one) * side
        for b in range(9):
            count = 1 << b
            group = min(count, 8)

            def level(i, _, b=b, count=count, group=group):
                n_i = jnp.int32(0)
                for bit in range(3, b):
                    n_i = n_i | (((i >> (bit - 3)) & 1) << tile_qubits[bit])
                for u in range(group):
                    n_u = sum(1 << tile_qubits[bit] for bit in range(3) if (u >> bit) & 1)
                    sel = ((n_i | n_u) >> partners[b]) & 1
                    t = i * group + u
                    fc, fs = fac_c[2 * b + sel], fac_s[2 * b + sel]
                    tc, ts = tab_c[t], tab_s[t]
                    tab_c[t + count] = tc * fc - ts * fs
                    tab_s[t + count] = ts * fc + tc * fs
                return 0

            lax.fori_loop(0, count // group, level, 0)

    lin_mid = [choose(PHASE_OUT, picks[0, q]) + choose(PHASE_IN, picks[1, q]) for q in range(25)]
    const_mid = functools.reduce(lambda a, b: a + b, [choose(PHASE_ALL, picks[0, q]) for q in range(25)])
    phase_table(0, me << 11, 18, lin_mid, const_mid, 2.0**-12)

    row_i = lax.broadcasted_iota(jnp.int32, (256, 128), 0)
    col_i = lax.broadcasted_iota(jnp.int32, (256, 128), 1)
    lanes_mat[...] = parity_sign(row_i & col_i & 127).astype(jnp.bfloat16)
    row_j = lax.broadcasted_iota(jnp.int32, (256, 256), 0)
    col_j = lax.broadcasted_iota(jnp.int32, (256, 256), 1)
    same = ((row_j ^ col_j) & 4) == 0
    rows_mat[...] = jnp.where(same, parity_sign(row_j & col_j & 251), 0.0).astype(jnp.bfloat16)

    def mix_lanes(value):
        return jnp.dot(split(value), lanes_mat[...], preferred_element_type=jnp.float32)

    def mix_rows(value):
        wide = jnp.dot(rows_mat[...], split(value), preferred_element_type=jnp.float32)
        return wide[:, :128] + wide[:, 128:]

    def middle(j):
        source, target = slot_of(0, 4, j), slot_of(1, 0, j)

        def before(x, _):
            value = st[source, x].reshape(256, 128)
            work[x] = mix_rows(mix_lanes(value)).reshape(4, 4, 2, 8, 128)
            return 0

        def between(i, _):
            for u in range(2):
                y, z, c = i // 4, i % 4, u
                tiles = hadamard([work[x, y, z, c] for x in range(4)])
                for x in range(4):
                    t = j * 128 + x * 32 + i * 2 + u
                    tiles[x] = tiles[x] * tab_c[t] + swap(tiles[x]) * tab_s[t]
                tiles = hadamard(tiles)
                for x in range(4):
                    work[x, y, z, c] = tiles[x]
            return 0

        def after(x, _):
            value = work[x].reshape(256, 128)
            st[target, x] = mix_lanes(mix_rows(value)).reshape(4, 4, 2, 8, 128)
            return 0

        lax.fori_loop(0, 4, before, 0)
        lax.fori_loop(0, 16, between, 0)
        lax.fori_loop(0, 4, after, 0)

    travel(0)
    for j in (2, 0, 1, 3):
        arrived_step(0, j, 3, 0)
        middle(j)
        for h in (1, 0):
            send_step(1, j, 0, h)

    lin_end = [choose(PHASE_OUT, picks[1, q]) for q in range(25)]
    const_end = functools.reduce(lambda a, b: a + b, [choose(PHASE_ALL, picks[1, q]) for q in range(25)])
    phase_table(1, me << 18, 11, lin_end, const_end, 2.0**-13)
    sent(0, range(4))

    travel(1)
    for n, j in enumerate((2, 0, 1, 3)):
        arrived_step(1, j, 3, 0)
        walsh_rows(slot_of(1, 4, j), n)

    tile_of = lax.broadcasted_iota(jnp.int32, (128, 1024), 1) >> 3
    number = functools.reduce(
        lambda a, b: a | b, [((tile_of >> b) & 1) << ROW_BITS[b] for b in range(7)]
    )
    pick_rows = (number == lax.broadcasted_iota(jnp.int32, (128, 1024), 0)).astype(jnp.float32).astype(jnp.bfloat16)
    wide = jnp.dot(pick_rows, split(acc[...].reshape(1024, 128)), preferred_element_type=jnp.float32)
    by_row = wide[:, :128] + wide[:, 128:]
    row_mass = jnp.sum(by_row.T, axis=0, keepdims=True)
    own_a = pos["z"] * 2 + pos["c"]
    mass_a[own_a] = jnp.broadcast_to(row_mass, (8, 128))
    for z in range(4):
        for c in range(2):
            if z or c:
                pltpu.make_async_remote_copy(
                    mass_a.at[own_a],
                    mass_a.at[own_a],
                    mass_send.at[0],
                    mass_recv.at[0],
                    device_id=moved(pos, z=z, c=c),
                    device_id_type=MESH,
                ).start()

    def last_rows(i, _):
        xh, z, y = i // 16, (i // 4) % 4, i % 4
        for xl in range(2):
            for c in range(2):
                m = i * 4 + xl * 2 + c
                x = 2 * xh + xl
                r = ((x * 4 + y) * 4 + z) * 2 + c
                tiles = hadamard([st[slot_of(1, 4, j), x, y, z, c] for j in range(CHUNKS)])
                for j in range(CHUNKS):
                    tiles[j] = tiles[j] * tab_c[j * 128 + r] + swap(tiles[j]) * tab_s[j * 128 + r]
                for t in range(2):
                    p0, p1 = tiles[2 * t], tiles[2 * t + 1]
                    vout[0, m, pl.ds(8 * t, 8)] = jnp.where(top, p0, swap(p1))
                    vout[1, m, pl.ds(8 * t, 8)] = jnp.where(top, swap(p0), p1)
        return 0

    def store(b):
        rows = pl.ds(b * 16, 16)
        return pltpu.make_async_copy(vout.at[:, rows], out_hbm.at[:, rows], out_sem.at[b])

    for b in range(4):
        lax.fori_loop(b * 4, b * 4 + 4, last_rows, 0)
        store(b).start()

    seven = mass_a.at[pl.ds(0, 7)]
    pltpu.make_async_copy(seven, seven, mass_recv.at[0]).wait()
    own_b = pos["x"] * 4 + pos["y"]
    mass_b[own_b] = jnp.sum(mass_a[...], axis=0)
    for x in range(4):
        for y in range(4):
            if x or y:
                pltpu.make_async_remote_copy(
                    mass_b.at[own_b],
                    mass_b.at[own_b],
                    mass_send.at[1],
                    mass_recv.at[1],
                    device_id=moved(pos, x=x, y=y),
                    device_id_type=MESH,
                ).start()

    for b in range(4, 8):
        lax.fori_loop(b * 4, b * 4 + 4, last_rows, 0)
        store(b).start()

    sent(1, range(4))
    fifteen = mass_b.at[pl.ds(0, 15)]
    pltpu.make_async_copy(fifteen, fifteen, mass_recv.at[1]).wait()
    total = jnp.sum(mass_b[...], axis=0) * (2.0**-42)
    marginal_ref[...] = total[0:1]
    pltpu.make_async_copy(seven, seven, mass_send.at[0]).wait()
    pltpu.make_async_copy(fifteen, fifteen, mass_send.at[1]).wait()
    for b in range(8):
        store(b).wait()


def shards(amplitudes, gate_picks, pair_qubits, angles):
    rows = amplitudes.reshape(2, 128, 16, 128)
    f32 = jnp.float32
    final, marginal = pl.pallas_call(
        kernel,
        out_shape=(
            jax.ShapeDtypeStruct((2, 128, 16, 128), f32),
            jax.ShapeDtypeStruct((1, 128), f32),
        ),
        in_specs=[
            pl.BlockSpec(memory_space=pl.ANY),
            pl.BlockSpec(memory_space=pltpu.SMEM),
            pl.BlockSpec(memory_space=pltpu.SMEM),
            pl.BlockSpec(memory_space=pltpu.SMEM),
        ],
        out_specs=(
            pl.BlockSpec(memory_space=pl.ANY),
            pl.BlockSpec(memory_space=pltpu.VMEM),
        ),
        scratch_shapes=[
            pltpu.VMEM((40, 4, 4, 4, 2, 8, 128), f32),
            pltpu.VMEM((2, 128, 16, 128), f32),
            pltpu.VMEM((2, 128, 16, 128), f32),
            pltpu.VMEM((512, 8, 128), f32),
            pltpu.VMEM((512, 8, 128), f32),
            pltpu.VMEM((8, 8, 128), f32),
            pltpu.VMEM((8, 8, 128), f32),
            pltpu.VMEM((18, 8, 128), f32),
            pltpu.VMEM((18, 8, 128), f32),
            pltpu.VMEM((4, 4, 4, 2, 8, 128), f32),
            pltpu.VMEM((4, 4, 4, 2, 8, 128), f32),
            pltpu.VMEM((256, 128), jnp.bfloat16),
            pltpu.VMEM((256, 256), jnp.bfloat16),
            pltpu.VMEM((8, 8, 128), f32),
            pltpu.VMEM((16, 8, 128), f32),
            pltpu.SemaphoreType.DMA((8,)),
            pltpu.SemaphoreType.DMA((8,)),
            pltpu.SemaphoreType.DMA((2, 4, 4)),
            pltpu.SemaphoreType.DMA((2, 4, 4, 2)),
            pltpu.SemaphoreType.DMA((2, 4)),
            pltpu.SemaphoreType.DMA((2,)),
            pltpu.SemaphoreType.DMA((2,)),
        ],
        compiler_params=pltpu.CompilerParams(
            collective_id=0, has_side_effects=True, vmem_limit_bytes=52 << 20
        ),
        name="circuit",
    )(rows, gate_picks, pair_qubits, angles)
    return final.reshape(2, 1, 262144), marginal.reshape(128)


def solution(mesh):
    placed = (P(None, ("hi", "lo"), None), P(), P(), P())
    return jax.shard_map(
        shards,
        mesh=mesh,
        in_specs=placed,
        out_specs=(P(None, ("hi", "lo"), None), P()),
        check_vma=False,
    )
```

profile of v0, /device:TPU:1, one launch (start us, length us, event | category | flops | bytes accessed | tf_op | source)
XLA Modules:
  0.0 85.9 jit_solution(914277419515118776)
XLA Ops:
  0.6 0.8 copy.6.pairs
  1.4 0.0 copy-start
  1.4 0.7 copy-done
  2.1 0.0 copy-start.1
  2.1 0.7 copy-done.1
  2.8 78.9 %circuit.1 = (f32[2,128,16,128]{3,2,1,0:T(8,128)}, f32[1,128]{1,0:T(1,128)S(1)}) custom-call(f32[2,128,16,128]{3,2,1,0:T(8,128)} %bitcast.4, s32[2,25]{1,0:T(2,128)S(1)} %copy-done, s32[2,10,2]{2,1,0:T(8,128)S(1)} %copy.6.pairs, f32[2,10]{1,0:T(2,128)S(1)} %copy-done.1), custom_call_target="tpu_custom_call" | custom-call | tf_op jit(solution)/shard_map/circuit/pallas_call | solution.py:469
  81.6 3.8 %copy.10 = f32[2,1,262144]{2,1,0:T(1,128)} copy(f32[2,1,262144]{2,1,0:T(1,128)} %bitcast.5) | data formatting | bytes 4194304
  85.4 0.5 copy.11
Async XLA Ops:
  1.4 0.7 copy-start
  2.1 0.7 copy-start.1
where the time goes:
time: 86.2 us; the launch traced here: 85.9 us
  Pallas kernels  78.9 us (92%)
  local copies, waits for them, and re-layouts  6.43 us (7%)
    pallas_call x1, Pallas kernels, shards(): pl.pallas_call(kernel, out_shape=(jax.ShapeDtypeStruct((2, 128, 16, 128),...  78.9 us
    unnamed x7, local copies, waits for them, and re-layouts  6.43 us

commit v1 on v0

--- a/solution.py
+++ b/solution.py
@@ -77,12 +77,15 @@
 
 def kernel(
     x_hbm,
+    picks_hbm,
+    pairs_hbm,
+    angles_hbm,
+    out_hbm,
+    marginal_ref,
+    st,
     picks,
     pairs,
     angles,
-    out_hbm,
-    marginal_ref,
-    st,
     vin,
     vout,
     tab_c,
@@ -95,9 +98,11 @@
     acc,
     lanes_mat,
     rows_mat,
+    pick_rows,
     mass_a,
     mass_b,
     in_sem,
+    small_sem,
     out_sem,
     send_sem,
     recv_sem,
@@ -112,8 +117,15 @@
         rows = pl.ds(b * 16, 16)
         return pltpu.make_async_copy(x_hbm.at[:, rows], vin.at[:, rows], in_sem.at[b])
 
+    small = [
+        pltpu.make_async_copy(source, target, small_sem.at[n])
+        for n, (source, target) in enumerate(((picks_hbm, picks), (pairs_hbm, pairs), (angles_hbm, angles)))
+    ]
+    small[0].start()
     for b in range(8):
         load(b).start()
+    small[1].start()
+    small[2].start()
 
     barrier = pltpu.get_barrier_semaphore()
     flips = [{"z": z, "c": c} for z in range(4) for c in range(2) if z or c]
@@ -128,6 +140,7 @@
     local_n = lane | ((sub & 3) << 7)
     eighth = math.pi / 4
 
+    small[0].wait()
     lin_in = [choose(PHASE_IN, picks[0, q]) for q in range(25)]
     n_first = local_n | (me << 18)
     turn = jnp.zeros((8, 128), jnp.int32)
@@ -268,11 +281,14 @@
         for h in (1, 0):
             send_step(0, j, 0, h)
 
+    small[1].wait()
+    small[2].wait()
+
     def phase_table(layer, n_base, row_base, linear, constant, scale):
         tile_qubits = [row_base + b for b in ROW_BITS] + list(CHUNK_QUBITS)
         other = [q for q in range(25) if q not in tile_qubits]
-        first = [pairs[layer, k, 0] for k in range(10)]
-        second = [pairs[layer, k, 1] for k in range(10)]
+        first = [pairs[layer, 0, k] for k in range(10)]
+        second = [pairs[layer, 1, k] for k in range(10)]
         theta = [angles[layer, k] for k in range(10)]
         n0 = local_n | n_base
         turns = jnp.full((8, 128), 0, jnp.int32) + constant
@@ -333,6 +349,12 @@
     same = ((row_j ^ col_j) & 4) == 0
     rows_mat[...] = jnp.where(same, parity_sign(row_j & col_j & 251), 0.0).astype(jnp.bfloat16)
 
+    tile_of = lax.broadcasted_iota(jnp.int32, (128, 1024), 1) >> 3
+    number = functools.reduce(
+        lambda a, b: a | b, [((tile_of >> b) & 1) << ROW_BITS[b] for b in range(7)]
+    )
+    pick_rows[...] = (number == lax.broadcasted_iota(jnp.int32, (128, 1024), 0)).astype(jnp.float32).astype(jnp.bfloat16)
+
     def mix_lanes(value):
         return jnp.dot(split(value), lanes_mat[...], preferred_element_type=jnp.float32)
 
@@ -365,9 +387,11 @@
             st[target, x] = mix_lanes(mix_rows(value)).reshape(4, 4, 2, 8, 128)
             return 0
 
-        lax.fori_loop(0, 4, before, 0)
+        for x in range(4):
+            before(x, 0)
         lax.fori_loop(0, 16, between, 0)
-        lax.fori_loop(0, 4, after, 0)
+        for x in range(4):
+            after(x, 0)
 
     travel(0)
     for j in (2, 0, 1, 3):
@@ -386,12 +410,7 @@
         arrived_step(1, j, 3, 0)
         walsh_rows(slot_of(1, 4, j), n)
 
-    tile_of = lax.broadcasted_iota(jnp.int32, (128, 1024), 1) >> 3
-    number = functools.reduce(
-        lambda a, b: a | b, [((tile_of >> b) & 1) << ROW_BITS[b] for b in range(7)]
-    )
-    pick_rows = (number == lax.broadcasted_iota(jnp.int32, (128, 1024), 0)).astype(jnp.float32).astype(jnp.bfloat16)
-    wide = jnp.dot(pick_rows, split(acc[...].reshape(1024, 128)), preferred_element_type=jnp.float32)
+    wide = jnp.dot(pick_rows[...], split(acc[...].reshape(1024, 128)), preferred_element_type=jnp.float32)
     by_row = wide[:, :128] + wide[:, 128:]
     row_mass = jnp.sum(by_row.T, axis=0, keepdims=True)
     own_a = pos["z"] * 2 + pos["c"]
@@ -463,20 +482,40 @@
         store(b).wait()
 
 
+def place(state, mass, out_state, out_mass, held, in_sem, out_sem):
+    def parts(n):
+        return (n % 2, pl.ds(n // 2 * 16, 16))
+
+    def fetch(n):
+        return pltpu.make_async_copy(state.at[parts(n)], held.at[parts(n)], in_sem.at[n])
+
+    def put(n):
+        return pltpu.make_async_copy(held.at[parts(n)], out_state.at[parts(n)], out_sem.at[n])
+
+    for n in range(16):
+        fetch(n).start()
+    out_mass[...] = mass[...]
+    for n in range(16):
+        fetch(n).wait()
+        put(n).start()
+    for n in range(16):
+        put(n).wait()
+
+
 def shards(amplitudes, gate_picks, pair_qubits, angles):
     rows = amplitudes.reshape(2, 128, 16, 128)
     f32 = jnp.float32
-    final, marginal = pl.pallas_call(
+    state, mass = pl.pallas_call(
         kernel,
         out_shape=(
             jax.ShapeDtypeStruct((2, 128, 16, 128), f32),
             jax.ShapeDtypeStruct((1, 128), f32),
         ),
         in_specs=[
-            pl.BlockSpec(memory_space=pl.ANY),
-            pl.BlockSpec(memory_space=pltpu.SMEM),
-            pl.BlockSpec(memory_space=pltpu.SMEM),
-            pl.BlockSpec(memory_space=pltpu.SMEM),
+            pl.BlockSpec(memory_space=pltpu.HBM),
+            pl.BlockSpec(memory_space=pltpu.HBM),
+            pl.BlockSpec(memory_space=pltpu.HBM),
+            pl.BlockSpec(memory_space=pltpu.HBM),
         ],
         out_specs=(
             pl.BlockSpec(memory_space=pl.ANY),
@@ -484,6 +523,9 @@
         ),
         scratch_shapes=[
             pltpu.VMEM((40, 4, 4, 4, 2, 8, 128), f32),
+            pltpu.SMEM((2, 25), jnp.int32),
+            pltpu.SMEM((2, 2, 10), jnp.int32),
+            pltpu.SMEM((2, 10), f32),
             pltpu.VMEM((2, 128, 16, 128), f32),
             pltpu.VMEM((2, 128, 16, 128), f32),
             pltpu.VMEM((512, 8, 128), f32),
@@ -496,9 +538,11 @@
             pltpu.VMEM((4, 4, 4, 2, 8, 128), f32),
             pltpu.VMEM((256, 128), jnp.bfloat16),
             pltpu.VMEM((256, 256), jnp.bfloat16),
+            pltpu.VMEM((128, 1024), jnp.bfloat16),
             pltpu.VMEM((8, 8, 128), f32),
             pltpu.VMEM((16, 8, 128), f32),
             pltpu.SemaphoreType.DMA((8,)),
+            pltpu.SemaphoreType.DMA((3,)),
             pltpu.SemaphoreType.DMA((8,)),
             pltpu.SemaphoreType.DMA((2, 4, 4)),
             pltpu.SemaphoreType.DMA((2, 4, 4, 2)),
@@ -507,10 +551,26 @@
             pltpu.SemaphoreType.DMA((2,)),
         ],
         compiler_params=pltpu.CompilerParams(
-            collective_id=0, has_side_effects=True, vmem_limit_bytes=52 << 20
+            collective_id=0, has_side_effects=True, vmem_limit_bytes=63 << 20
         ),
         name="circuit",
-    )(rows, gate_picks, pair_qubits, angles)
+    )(rows, gate_picks, pair_qubits.transpose(0, 2, 1), angles)
+    final, marginal = pl.pallas_call(
+        place,
+        out_shape=(
+            jax.ShapeDtypeStruct((2, 128, 16, 128), f32),
+            jax.ShapeDtypeStruct((1, 128), f32),
+        ),
+        in_specs=[pl.BlockSpec(memory_space=pl.ANY), pl.BlockSpec(memory_space=pltpu.VMEM)],
+        out_specs=(pl.BlockSpec(memory_space=pl.ANY), pl.BlockSpec(memory_space=pltpu.VMEM)),
+        scratch_shapes=[
+            pltpu.VMEM((2, 128, 16, 128), f32),
+            pltpu.SemaphoreType.DMA((16,)),
+            pltpu.SemaphoreType.DMA((16,)),
+        ],
+        compiler_params=pltpu.CompilerParams(vmem_limit_bytes=63 << 20),
+        name="place",
+    )(state, mass)
     return final.reshape(2, 1, 262144), marginal.reshape(128)
 
 

time: 86.2 us -> 79.8 us (0.926)
  local copies, waits for them, and re-layouts: 6.43 us -> 0 us
    unnamed x7 -> x0, local copies, waits for them, and re-layouts: 6.43 us -> none
    pallas_call x0 -> x1, Pallas kernels: none -> 3.69 us  [shards(): pl.pallas_call(place, out_shape=(jax.ShapeDtypeStruct((2, 128, 16, 128),...]
    pallas_call x1, Pallas kernels: 78.9 us -> 75.3 us  [shards(): pl.pallas_call(kernel, out_shape=(jax.ShapeDtypeStruct((2, 128, 16, 128),...]
where the time goes in v1:
time: 79.8 us; the launch traced here: 79.6 us
  Pallas kernels  79 us (99%)
    pallas_call x1, Pallas kernels, shards(): pl.pallas_call(kernel, out_shape=(jax.ShapeDtypeStruct((2, 128, 16, 128),...  75.3 us
    pallas_call x1, Pallas kernels, shards(): pl.pallas_call(place, out_shape=(jax.ShapeDtypeStruct((2, 128, 16, 128),...  3.69 us

profile of v1, /device:TPU:1, one launch (start us, length us, event | category | flops | bytes accessed | tf_op | source)
XLA Modules:
  0.0 79.6 jit_solution(7730017058891166656)
XLA Ops:
  0.6 75.3 %circuit.1 = (f32[2,128,16,128]{3,2,1,0:T(8,128)}, f32[1,128]{1,0:T(1,128)}) custom-call(f32[2,128,16,128]{3,2,1,0:T(8,128)} %bitcast.4, s32[2,25]{1,0:T(2,128)} %picks_hbm.1, s32[2,2,10]{2,1,0:T(2,128)} %bitcast.5, f32[2,10]{1,0:T(2,128)} %angles_hbm.1), custom_call_target="tpu_custom_call" | custom-call | tf_op jit(solution)/shard_map/circuit/pallas_call | solution.py:508
  75.9 3.7 %place.1 = (f32[2,128,16,128]{3,2,1,0:T(8,128)}, f32[1,128]{1,0:T(1,128)}) custom-call(f32[2,128,16,128]{3,2,1,0:T(8,128)} %get-tuple-element.6.state, f32[1,128]{1,0:T(1,128)} %get-tuple-element.7.mass), custom_call_target="tpu_custom_call" | custom-call | tf_op jit(solution)/shard_map/place/pallas_call | solution.py:558

commit v2 on v1

--- a/solution.py
+++ b/solution.py
@@ -180,7 +180,7 @@
 
     for b in range(8):
         load(b).wait()
-        lax.fori_loop(b * 4, b * 4 + 4, first_rows, 0)
+        lax.fori_loop(b * 4, b * 4 + 4, first_rows, 0, unroll=2)
 
     def walsh_rows(slot, mass=None):
         def pass_xy(i, _):
@@ -204,8 +204,8 @@
                         acc[x, y, z, c] = acc[x, y, z, c] + tile * tile
             return 0
 
-        lax.fori_loop(0, 8, pass_xy, 0)
-        lax.fori_loop(0, 16, pass_zc, 0)
+        lax.fori_loop(0, 8, pass_xy, 0, unroll=2)
+        lax.fori_loop(0, 16, pass_zc, 0, unroll=4)
 
     def slot_of(e, i, j):
         return e * 20 + i * 4 + j
@@ -219,7 +219,7 @@
         a = ORDER[j][i]
         if i < 3:
             d, piece = half(j, h)
-            for flip in range(SIZE[a]):
+            for flip in ((2, 1, 3, 0) if SIZE[a] == 4 else (1, 0)):
                 target = jnp.bitwise_xor(pos[a], flip) if flip else pos[a]
                 src = part(st, slot_of(e, i, j), {a: target, d: piece})
                 dst = part(st, slot_of(e, i + 1, j), {a: pos[a], d: piece})
@@ -233,7 +233,7 @@
                         device_id_type=MESH,
                     ).start()
                 else:
-                    pltpu.make_async_copy(src, dst, recv_sem.at[e, j, i, h]).start()
+                    dst[...] = src[...]
         else:
             width = SIZE[a] // 2
             for flip in range(h * width, h * width + width):
@@ -250,15 +250,17 @@
                         device_id_type=MESH,
                     ).start()
                 else:
-                    pltpu.make_async_copy(src, dst, last_sem.at[e, j]).start()
+                    dst[...] = src[...]
 
     def arrived_step(e, j, i, h):
+        a = ORDER[j][i]
+        rest = {a: pl.ds(0, SIZE[a] - 1)}
         if i < 3:
             d, piece = half(j, h)
-            ref = part(st, slot_of(e, i + 1, j), {d: piece})
+            ref = part(st, slot_of(e, i + 1, j), {**rest, d: piece})
             pltpu.make_async_copy(ref, ref, recv_sem.at[e, j, i, h]).wait()
         else:
-            ref = st.at[slot_of(e, 4, j)]
+            ref = part(st, slot_of(e, 4, j), rest)
             pltpu.make_async_copy(ref, ref, last_sem.at[e, j]).wait()
 
     def sent(e, steps):
@@ -389,7 +391,7 @@
 
         for x in range(4):
             before(x, 0)
-        lax.fori_loop(0, 16, between, 0)
+        lax.fori_loop(0, 16, between, 0, unroll=4)
         for x in range(4):
             after(x, 0)
 
@@ -448,7 +450,7 @@
         return pltpu.make_async_copy(vout.at[:, rows], out_hbm.at[:, rows], out_sem.at[b])
 
     for b in range(4):
-        lax.fori_loop(b * 4, b * 4 + 4, last_rows, 0)
+        lax.fori_loop(b * 4, b * 4 + 4, last_rows, 0, unroll=2)
         store(b).start()
 
     seven = mass_a.at[pl.ds(0, 7)]
@@ -468,7 +470,7 @@
                 ).start()
 
     for b in range(4, 8):
-        lax.fori_loop(b * 4, b * 4 + 4, last_rows, 0)
+        lax.fori_loop(b * 4, b * 4 + 4, last_rows, 0, unroll=2)
         store(b).start()
 
     sent(1, range(4))

time: 79.8 us -> 77.9 us (0.976)
  Pallas kernels: 79 us -> 77.1 us
    pallas_call x1, Pallas kernels: 75.3 us -> 73.4 us  [shards(): pl.pallas_call(kernel, out_shape=(jax.ShapeDtypeStruct((2, 128, 16, 128),...]
where the time goes in v2:
time: 77.9 us; the launch traced here: 77.7 us
  Pallas kernels  77.1 us (99%)
    pallas_call x1, Pallas kernels, shards(): pl.pallas_call(kernel, out_shape=(jax.ShapeDtypeStruct((2, 128, 16, 128),...  73.4 us
    pallas_call x1, Pallas kernels, shards(): pl.pallas_call(place, out_shape=(jax.ShapeDtypeStruct((2, 128, 16, 128),...  3.69 us

profile of v2, /device:TPU:1, one launch (start us, length us, event | category | flops | bytes accessed | tf_op | source)
XLA Modules:
  0.0 77.7 jit_solution(8827481430520473779)
XLA Ops:
  0.6 73.4 %circuit.1 = (f32[2,128,16,128]{3,2,1,0:T(8,128)}, f32[1,128]{1,0:T(1,128)}) custom-call(f32[2,128,16,128]{3,2,1,0:T(8,128)} %bitcast.4, s32[2,25]{1,0:T(2,128)} %picks_hbm.1, s32[2,2,10]{2,1,0:T(2,128)} %bitcast.5, f32[2,10]{1,0:T(2,128)} %angles_hbm.1), custom_call_target="tpu_custom_call" | custom-call | tf_op jit(solution)/shard_map/circuit/pallas_call | solution.py:510
  74.0 3.7 %place.1 = (f32[2,128,16,128]{3,2,1,0:T(8,128)}, f32[1,128]{1,0:T(1,128)}) custom-call(f32[2,128,16,128]{3,2,1,0:T(8,128)} %get-tuple-element.6.state, f32[1,128]{1,0:T(1,128)} %get-tuple-element.7.mass), custom_call_target="tpu_custom_call" | custom-call | tf_op jit(solution)/shard_map/place/pallas_call | solution.py:560

commit v3 on v2

--- a/solution.py
+++ b/solution.py
@@ -280,8 +280,9 @@
     pl.semaphore_wait(barrier, len(flips))
     for j in range(CHUNKS):
         walsh_rows(j)
-        for h in (1, 0):
-            send_step(0, j, 0, h)
+        send_step(0, j, 0, 1)
+    for j in range(CHUNKS):
+        send_step(0, j, 0, 0)
 
     small[1].wait()
     small[2].wait()

time: 77.9 us -> 77.4 us (level)
  no operation moved by 1% of the time
where the time goes in v3:
time: 77.4 us; the launch traced here: 77.2 us
  Pallas kernels  76.6 us (99%)
    pallas_call x1, Pallas kernels, shards(): pl.pallas_call(kernel, out_shape=(jax.ShapeDtypeStruct((2, 128, 16, 128),...  72.9 us
    pallas_call x1, Pallas kernels, shards(): pl.pallas_call(place, out_shape=(jax.ShapeDtypeStruct((2, 128, 16, 128),...  3.69 us

profile of v3, /device:TPU:1, one launch (start us, length us, event | category | flops | bytes accessed | tf_op | source)
XLA Modules:
  0.0 77.2 jit_solution(16184173970150753785)
XLA Ops:
  0.6 72.9 %circuit.1 = (f32[2,128,16,128]{3,2,1,0:T(8,128)}, f32[1,128]{1,0:T(1,128)}) custom-call(f32[2,128,16,128]{3,2,1,0:T(8,128)} %bitcast.4, s32[2,25]{1,0:T(2,128)} %picks_hbm.1, s32[2,2,10]{2,1,0:T(2,128)} %bitcast.5, f32[2,10]{1,0:T(2,128)} %angles_hbm.1), custom_call_target="tpu_custom_call" | custom-call | tf_op jit(solution)/shard_map/circuit/pallas_call | solution.py:511
  73.5 3.7 %place.1 = (f32[2,128,16,128]{3,2,1,0:T(8,128)}, f32[1,128]{1,0:T(1,128)}) custom-call(f32[2,128,16,128]{3,2,1,0:T(8,128)} %get-tuple-element.6.state, f32[1,128]{1,0:T(1,128)} %get-tuple-element.7.mass), custom_call_target="tpu_custom_call" | custom-call | tf_op jit(solution)/shard_map/place/pallas_call | solution.py:561

commit v4 on v3

--- a/solution.py
+++ b/solution.py
@@ -157,6 +157,7 @@
     def first_rows(i, _):
         xh, z, y = i // 16, (i // 4) % 4, i % 4
         k0 = xh * lin_in[17] + (z // 2) * lin_in[16] + (z % 2) * lin_in[15] + (y // 2) * lin_in[14] + (y % 2) * lin_in[13]
+        rows = []
         for xl in range(2):
             for c in range(2):
                 m = i * 4 + xl * 2 + c
@@ -173,9 +174,11 @@
                         else:
                             p, pr = jnp.where(top, rre, im), jnp.where(top, rim, re)
                         tiles.append(p * in_c[k] + pr * in_s[k])
-                tiles = hadamard(tiles)
-                for j in range(CHUNKS):
-                    st[j, 2 * xh + xl, y, z, c] = tiles[j]
+                rows.append(hadamard(tiles))
+        for j in range(CHUNKS):
+            tiles = hadamard([row[j] for row in rows])
+            for n in range(4):
+                st[j, 2 * xh + n // 2, y, z, n % 2] = tiles[n]
         return 0
 
     for b in range(8):
@@ -206,6 +209,16 @@
 
         lax.fori_loop(0, 8, pass_xy, 0, unroll=2)
         lax.fori_loop(0, 16, pass_zc, 0, unroll=4)
+
+    def walsh_first(slot):
+        def rest(i, _):
+            places = [(2 * xh + i // 2, y, z, i % 2) for xh in range(2) for y in range(4) for z in range(4)]
+            tiles = hadamard([st[(slot,) + place] for place in places])
+            for place, tile in zip(places, tiles):
+                st[(slot,) + place] = tile
+            return 0
+
+        lax.fori_loop(0, 4, rest, 0)
 
     def slot_of(e, i, j):
         return e * 20 + i * 4 + j
@@ -279,7 +292,7 @@
 
     pl.semaphore_wait(barrier, len(flips))
     for j in range(CHUNKS):
-        walsh_rows(j)
+        walsh_first(j)
         send_step(0, j, 0, 1)
     for j in range(CHUNKS):
         send_step(0, j, 0, 0)

time: 77.4 us -> 77 us (level)
  no operation moved by 1% of the time
where the time goes in v4:
time: 77 us; the launch traced here: 76.8 us
  Pallas kernels  76.2 us (99%)
    pallas_call x1, Pallas kernels, shards(): pl.pallas_call(kernel, out_shape=(jax.ShapeDtypeStruct((2, 128, 16, 128),...  72.5 us
    pallas_call x1, Pallas kernels, shards(): pl.pallas_call(place, out_shape=(jax.ShapeDtypeStruct((2, 128, 16, 128),...  3.69 us

profile of v4, /device:TPU:1, one launch (start us, length us, event | category | flops | bytes accessed | tf_op | source)
XLA Modules:
  0.0 76.8 jit_solution(17658683947774366572)
XLA Ops:
  0.6 72.5 %circuit.1 = (f32[2,128,16,128]{3,2,1,0:T(8,128)}, f32[1,128]{1,0:T(1,128)}) custom-call(f32[2,128,16,128]{3,2,1,0:T(8,128)} %bitcast.4, s32[2,25]{1,0:T(2,128)} %picks_hbm.1, s32[2,2,10]{2,1,0:T(2,128)} %bitcast.5, f32[2,10]{1,0:T(2,128)} %angles_hbm.1), custom_call_target="tpu_custom_call" | custom-call | tf_op jit(solution)/shard_map/circuit/pallas_call | solution.py:524
  73.2 3.7 %place.1 = (f32[2,128,16,128]{3,2,1,0:T(8,128)}, f32[1,128]{1,0:T(1,128)}) custom-call(f32[2,128,16,128]{3,2,1,0:T(8,128)} %get-tuple-element.6.state, f32[1,128]{1,0:T(1,128)} %get-tuple-element.7.mass), custom_call_target="tpu_custom_call" | custom-call | tf_op jit(solution)/shard_map/place/pallas_call | solution.py:574
